TPU v7x, 256 devices: a whole 4x4x8 slice. The times are simulated.
256 devices in a mesh: row: 32 (over x, y, core), col: 8 (over z).
Axes of the slice: x: 4, y: 4, z: 8, core: 2. Of those that a mesh axis runs over, the one named last changes fastest.
Arguments:
- tokens: bfloat16 [1024, 12288], P('row', 'col'), may hold values from -6 to 6
- weight: bfloat16 [12288, 49152], P('col', 'row'), may hold values from -0.0546875 to 0.0546875
- grad_out: bfloat16 [1024, 49152], P('col', 'row'), may hold values from -6 to 6
Outputs:
- hidden: bfloat16 [1024, 49152], P('col', 'row')
- grad_tokens: bfloat16 [1024, 12288], P('row', 'col')
- grad_weight: bfloat16 [12288, 49152], P('col', 'row')
All inputs are finite; a program needn't handle non-finite values.
Results may differ from a plain program's by a relative error of at most 0.024.
Values may be sent and summed in bfloat16 or wider, within the bound.
A program may use at most 64 MiB of HBM per device.

v0:
```python
import math

import jax
import jax.numpy as jnp
from jax import lax
from jax.sharding import PartitionSpec as P


def activations(pre):
    coef = math.sqrt(2.0 / math.pi)
    inner = coef * (pre + 0.044715 * pre * pre * pre)
    tval = jnp.tanh(inner)
    hidden = 0.5 * pre * (1.0 + tval)
    slope = 0.5 * (1.0 + tval) + 0.5 * pre * (1.0 - tval * tval) * coef * (
        1.0 + 3.0 * 0.044715 * pre * pre
    )
    return (hidden, slope)


def rounded(value):
    return lax.optimization_barrier(value.astype(jnp.bfloat16)).astype(jnp.float32)


def times_transposed(left, right):
    return lax.dot_general(
        left, right, (((1,), (1,)), ((), ())), preferred_element_type=jnp.float32
    )


def over_tokens(left, right):
    return lax.dot_general(
        left, right, (((0,), (0,)), ((), ())), preferred_element_type=jnp.float32
    )


def local(tokens, weight, grad_out):
    all_tokens = lax.all_gather(tokens, "row", axis=0, tiled=True)
    rows = all_tokens
    pre = lax.psum_scatter(
        rounded(jnp.dot(rows, weight, preferred_element_type=jnp.float32)).astype(jnp.bfloat16),
        "col",
        scatter_dimension=0,
        tiled=True,
    ).astype(jnp.float32)
    hidden, slope = activations(pre)
    grad_pre = (grad_out.astype(jnp.float32) * slope).astype(jnp.bfloat16)
    all_grads = lax.all_gather(grad_pre, "col", axis=0, tiled=True)
    rows = all_grads
    grad_tokens = lax.psum_scatter(
        rounded(times_transposed(rows, weight)).astype(jnp.bfloat16),
        "row",
        scatter_dimension=0,
        tiled=True,
    )
    grad_weight = over_tokens(all_tokens, all_grads)
    return (hidden.astype(jnp.bfloat16), grad_tokens, grad_weight.astype(jnp.bfloat16))


def solution(mesh):
    placed = (P("row", "col"), P("col", "row"), P("col", "row"))
    return jax.shard_map(
        local,
        mesh=mesh,
        in_specs=placed,
        out_specs=(P("col", "row"), P("row", "col"), P("col", "row")),
        check_vma=False,
    )
```

profile of v0, /device:TPU:3, one launch (start us, length us, event | category | flops | bytes accessed | tf_op | source)
XLA Modules:
  0.0 266.4 jit_solution(9001218032549255396)
XLA Ops:
  7.2 0.0 all-gather.3.cloned.1.call-start
  7.2 0.7 all-gather.3.cloned.1.call-update
  7.9 0.0 reduce-scatter.3.cloned.1.call-start
  7.9 55.7 %all-gather.3.cloned.1.call-done = bf16[1024,1536]{1,0:T(8,128)(2,1)} async-done(((bf16[32,1536]{1,0:T(8,128)(2,1)}), bf16[1024,1536]{1,0:T(8,128)(2,1)}) %all-gather.3.cloned.1.call-update) | async-done | bytes 3145744 | tf_op jit(solution)/shard_map/all_gather | solution.py:37
  63.6 9.2 %convolution_convert_fusion.2 = bf16[1024,1536]{1,0:T(8,128)(2,1)} fusion(bf16[1024,1536]{1,0:T(8,128)(2,1)} %all-gather.3.cloned.1.call-done, bf16[1536,1536]{1,0:T(8,128)(2,1)} %param.4), kind=kOutput, calls=%fused_computation.3 | convolution fusion | flops 4833411072 | bytes 11010048 | tf_op jit(solution)/shard_map/dot_general | solution.py:40
  72.8 0.0 copy-start
  72.8 0.0 reduce-scatter.3.cloned.1.call-update
  72.8 0.0 all-gather.5.cloned.1.call-start
  72.9 43.7 %reduce-scatter.3.cloned.1.call-done = bf16[128,1536]{1,0:T(8,128)(2,1)} async-done(((bf16[1024,1536]{1,0:T(8,128)(2,1)}), bf16[128,1536]{1,0:T(8,128)(2,1)}) %reduce-scatter.3.cloned.1.call-update) | async-done | bytes 393232 | tf_op jit(solution)/shard_map/reduce_scatter | solution.py:39
  116.6 0.0 copy-done
  116.6 2.5 fusion.8
  119.0 0.0 all-gather.5.cloned.1.call-update
  119.0 0.0 reduce-scatter.5.cloned.1.call-start
  119.1 46.7 %all-gather.5.cloned.1.call-done = bf16[1024,1536]{1,0:T(8,128)(2,1)} async-done(((bf16[128,1536]{1,0:T(8,128)(2,1)}), bf16[1024,1536]{1,0:T(8,128)(2,1)}) %all-gather.5.cloned.1.call-update) | async-done | bytes 3145744 | tf_op jit(solution)/shard_map/all_gather | solution.py:47
  165.8 9.2 %convolution_convert_fusion.1 = bf16[1024,1536]{1,0:T(8,128)(2,1)} fusion(bf16[1024,1536]{1,0:T(8,128)(2,1)} %all-gather.5.cloned.1.call-done, bf16[1536,1536]{1,0:T(8,128)(2,1)} %param.4), kind=kOutput, calls=%fused_computation.2 | convolution fusion | flops 4833411072 | bytes 11010048 | tf_op jit(solution)/shard_map/dot_general | solution.py:25
  175.1 0.0 copy-start.1
  175.1 0.0 reduce-scatter.5.cloned.1.call-update
  175.1 1.9 copy-done.1
  177.0 8.7 %fusion = bf16[1536,1536]{0,1:T(8,128)(2,1)} fusion(bf16[1024,1536]{1,0:T(8,128)(2,1)} %all-gather.5.cloned.1.call-done, bf16[1024,1536]{1,0:T(8,128)(2,1)S(1)} %copy-done.1), kind=kOutput, calls=%fused_computation.1 | convolution fusion | flops 4834197504 | bytes 11010048 | tf_op jit(solution)/shard_map/dot_general | solution.py:31
  185.7 6.7 %copy.6 = bf16[1536,1536]{1,0:T(8,128)(2,1)} copy(bf16[1536,1536]{0,1:T(8,128)(2,1)} %fusion) | data formatting | bytes 9437184
  192.4 67.5 %reduce-scatter.5.cloned.1.call-done = bf16[32,1536]{1,0:T(8,128)(2,1)} async-done(((bf16[1024,1536]{1,0:T(8,128)(2,1)}), bf16[32,1536]{1,0:T(8,128)(2,1)}) %reduce-scatter.5.cloned.1.call-update) | async-done | bytes 98320 | tf_op jit(solution)/shard_map/reduce_scatter | solution.py:49
Async XLA Ops:
  7.2 56.5 %all-gather.3.cloned.1.call-start = ((), (), s32[]{:S(2)}) async-start(), calls=%async_computation.2 | async-start | bytes 3244032 | tf_op jit(solution)/shard_map/all_gather | solution.py:37
  7.9 108.7 %reduce-scatter.3.cloned.1.call-start = ((), (), s32[]{:S(2)}) async-start(), calls=%async_computation.3 | async-start | bytes 3538944 | tf_op jit(solution)/shard_map/reduce_scatter | solution.py:39
  72.8 43.7 %copy-start = (bf16[128,1536]{1,0:T(8,128)(2,1)S(1)}, bf16[128,1536]{1,0:T(8,128)(2,1)}, u32[]{:S(2)}) copy-start(bf16[128,1536]{1,0:T(8,128)(2,1)} %param.5) | copy-start | bytes 1179652
  72.8 93.0 %all-gather.5.cloned.1.call-start = ((), (), s32[]{:S(2)}) async-start(), calls=%async_computation.4 | async-start | bytes 3538944 | tf_op jit(solution)/shard_map/all_gather | solution.py:47
  119.0 140.8 %reduce-scatter.5.cloned.1.call-start = ((), (), s32[]{:S(2)}) async-start(), calls=%async_computation.5 | async-start | bytes 3244032 | tf_op jit(solution)/shard_map/reduce_scatter | solution.py:49
  175.1 1.9 copy-start.1
Sparse Core Ops, SparseCore 0:
  10.5 53.0 all-gather.2
  73.0 43.5 reduce-scatter.2
  119.2 46.6 all-gather.4
  175.2 84.5 reduce-scatter.4
where the time goes:
time: 269 us; the launch traced here: 266 us
  waiting for transfers between devices  214 us (80%)
  matrix products  27.2 us (10%)
  between operations  13.8 us (5%)
  local copies, waits for them, and re-layouts  8.53 us (3%)
    reduce_scatter x1, waiting for transfers between devices, local(): lax.psum_scatter(rounded(times_transposed(rows, weight)).astype(jnp.bfloa...  67.5 us
    all_gather x1, waiting for transfers between devices, local(): all_tokens = lax.all_gather(tokens, 'row', axis=0, tiled=True)  55.7 us
    all_gather x1, waiting for transfers between devices, local(): all_grads = lax.all_gather(grad_pre, 'col', axis=0, tiled=True)  46.7 us
    reduce_scatter x1, waiting for transfers between devices, local(): lax.psum_scatter(rounded(jnp.dot(rows, weight, preferred_element_type=jnp...  43.7 us
    dot_general x1, matrix products, times_transposed(): lax.dot_general(left, right, (((1,), (1,)), ((), ())), preferred_element_...  9.25 us
    dot_general x1, matrix products, local(): jnp.dot(rows, weight, preferred_element_type=jnp.float32)  9.18 us
    dot_general x1, matrix products, over_tokens(): lax.dot_general(left, right, (((0,), (0,)), ((), ())), preferred_element_...  8.74 us
    unnamed x5, local copies, waits for them, and re-layouts  8.53 us
  transfers between devices with their start and end apart: 4, of which 4 were waited for; matrix products, arithmetic and copies ran while one was open for 6% of the time, Pallas kernels for 0%

commit v1 on v0

v1 whole, which is shorter than its diff:
```python
import math

import jax
import jax.numpy as jnp
from jax import lax
from jax.experimental import pallas as pl
from jax.experimental.pallas import tpu as pltpu
from jax.sharding import PartitionSpec as P

MESH = pl.DeviceIdType.MESH
F32 = jnp.float32
BF16 = jnp.bfloat16
NZ = 8
NC = 8
TB = 16
AHEAD = 1


def activations(pre):
    coef = math.sqrt(2.0 / math.pi)
    inner = coef * (pre + 0.044715 * pre * pre * pre)
    tval = jnp.tanh(inner)
    hidden = 0.5 * pre * (1.0 + tval)
    slope = 0.5 * (1.0 + tval) + 0.5 * pre * (1.0 - tval * tval) * coef * (
        1.0 + 3.0 * 0.044715 * pre * pre
    )
    return (hidden, slope)


def kernel(
    tok_in, w_in, go_in,
    hid_out, gt_out, gw_out,
    w, go, tok, part, ring, gath, quo, quo_in, rs_in, acc,
    tok_send, tok_recv, fwd_send, ring_send, ring_recv, gath_send, gath_recv,
    quo_send, quo_recv, rs_send, rs_recv, load_sem,
):
    row = lax.axis_index("row")
    z = lax.axis_index("col")
    core = lax.rem(row, 2)
    chip = row // 2
    x, y = chip // 4, lax.rem(chip, 4)
    d_me, r_me = row // 4, lax.rem(row, 4)
    sibling = (row + 1 - 2 * core, z)
    hops = ((row, lax.rem(z + 1, NZ)), (row, lax.rem(z + NZ - 1, NZ)))
    dm = tok.shape[-1]
    ff = gath.shape[-1]
    half = ff // 2

    load_w = pltpu.make_async_copy(w_in, w, load_sem.at[0])
    load_go = pltpu.make_async_copy(go_in, go, load_sem.at[1])
    load_w.start()
    load_go.start()

    def plane(j):
        px = lax.rem(x + j // 4, 4)
        py = lax.rem(y + lax.rem(j, 4), 4)
        return ((px * 4 + py) * 2 + core, z)

    barrier = pltpu.get_barrier_semaphore()
    for there in (*hops, sibling):
        pl.semaphore_signal(barrier, inc=1, device_id=there, device_id_type=MESH)

    def greet(j, _):
        pl.semaphore_signal(barrier, inc=1, device_id=plane(j), device_id_type=MESH)
        return 0

    lax.fori_loop(1, 16, greet, 0)
    pl.semaphore_wait(barrier, 18)

    def remote(src, dst, send, recv, there):
        return pltpu.make_async_remote_copy(
            src_ref=src, dst_ref=dst, send_sem=send, recv_sem=recv,
            device_id=there, device_id_type=MESH,
        )

    def send_tokens(c):
        h = c // 4

        @pl.when(r_me == lax.rem(c, 4))
        def _():
            mine = tok_in.at[pl.ds(pl.multiple_of(h * TB, TB), TB)]

            def one(j, _):
                remote(mine, tok.at[c, d_me], tok_send.at[h], tok_recv.at[c], plane(j)).start()
                return 0

            lax.fori_loop(1, 16, one, 0)
            pltpu.make_async_copy(mine, tok.at[c, d_me], tok_recv.at[c]).start()

    def forward_tokens(c):
        return remote(tok.at[c], tok.at[c], fwd_send.at[c], tok_recv.at[c], sibling)

    def ring_copy(d, c, s):
        if s == 0:
            cols = pl.ds(d * half, half)
            src = part.at[c, lax.rem(z + 4, NZ), :, cols]
            dst = ring.at[d, c, 0, :, cols]
        else:
            src, dst = ring.at[d, c, s - 1], ring.at[d, c, s]
        return remote(src, dst, ring_send.at[d, c, s], ring_recv.at[d, c, s], hops[d])

    def gath_copy(d, c, s):
        slot = lax.rem(z + (NZ - s if d == 0 else s), NZ)
        if s == 3:
            ref = gath.at[c, slot, :, pl.ds(d * half, half)]
        else:
            ref = gath.at[c, slot]
        return remote(ref, ref, gath_send.at[d, c, s], gath_recv.at[d, c, s], hops[d])

    def first(c):
        pltpu.make_async_copy(tok.at[c], tok.at[c], tok_recv.at[c]).wait()

        @pl.when(core == lax.rem(c, 2))
        def _():
            forward_tokens(c).start()

        @pl.when(c + AHEAD < NC)
        def _():
            send_tokens(c + AHEAD)

        @pl.when(c == 0)
        def _():
            load_w.wait()

        left = tok[c].reshape(NZ * TB, dm)

        def cols(n, _):
            at = pl.ds(pl.multiple_of(n * 256, 256), 256)
            got = jnp.dot(left, w[:, at], preferred_element_type=F32)
            part[c, :, :, at] = got.astype(BF16).reshape(NZ, TB, 256)
            return 0

        lax.fori_loop(0, ff // 256, cols, 0)
        for d in range(2):
            ring_copy(d, c, 0).start()

    def ring_step(c, s):
        for d in range(2):
            ring_copy(d, c, s - 1).wait_recv()
            at = lax.rem(z + (4 - s if d == 0 else 4 + s), NZ)
            if s == 1:
                got, rest = slice(d * half, (d + 1) * half), slice((1 - d) * half, (2 - d) * half)
                total = ring[d, c, 0, :, got].astype(F32) + part[c, at, :, got].astype(F32)
                ring[d, c, 0, :, got] = total.astype(BF16)
                ring[d, c, 0, :, rest] = part[c, at, :, rest]
            else:
                total = ring[d, c, s - 1].astype(F32) + part[c, at].astype(F32)
                ring[d, c, s - 1] = total.astype(BF16)
            ring_copy(d, c, s).start()

    def middle(c):
        @pl.when(c == 0)
        def _():
            load_go.wait()

        for d in range(2):
            ring_copy(d, c, 3).wait_recv()
        at = pl.ds(pl.multiple_of(lax.rem(c, 4) * 32 + (c // 4) * TB, TB), TB)
        pre = (
            part[c, z].astype(F32) + ring[0, c, 3].astype(F32) + ring[1, c, 3].astype(F32)
        )
        hidden, slope = activations(pre)
        hid_out[at, :] = hidden.astype(BF16)
        gath[c, z] = (go[at, :].astype(F32) * slope).astype(BF16)
        for d in range(2):
            gath_copy(d, c, 0).start()

    def gath_step(c, s):
        for d in range(2):
            gath_copy(d, c, s - 1).wait_recv()
            gath_copy(d, c, s).start()

    def quo_copy(c):
        return remote(quo.at[c], quo_in.at[c], quo_send.at[c], quo_recv.at[c], sibling)

    def back(c):
        for d in range(2):
            gath_copy(d, c, 3).wait_recv()
        left = gath[c].reshape(NZ * TB, ff)

        def cols(n, _):
            at = pl.ds(pl.multiple_of(n * 256, 256), 256)
            got = lax.dot_general(
                left, w[at, :], (((1,), (1,)), ((), ())), preferred_element_type=F32
            )
            quo[c, :, :, at] = got.astype(BF16).reshape(NZ, TB, 256)
            return 0

        lax.fori_loop(0, dm // 256, cols, 0)

        @pl.when(core != lax.rem(c, 2))
        def _():
            quo_copy(c).start()

    def scatter(c):
        r, h = lax.rem(c, 4), c // 4

        @pl.when(core == lax.rem(c, 2))
        def _():
            quo_copy(c).wait_recv()

            def one(j, _):
                at = lax.rem(d_me + j, NZ)
                total = quo[c, at].astype(F32) + quo_in[c, at].astype(F32)
                quo[c, at] = total.astype(BF16)
                there = at * 4 + r

                @pl.when(there != row)
                def _():
                    remote(
                        quo.at[c, at], rs_in.at[h, chip], rs_send.at[c], rs_recv.at[h], (there, z)
                    ).start()

                @pl.when(there == row)
                def _():
                    pltpu.make_async_copy(quo.at[c, at], rs_in.at[h, chip], rs_recv.at[h]).start()

                return 0

            lax.fori_loop(0, NZ, one, 0)

    def weigh(c, n, opening, closing):
        left = tok[pl.ds(c, n)].reshape(n * NZ * TB, dm)
        right = gath[pl.ds(c, n)].reshape(n * NZ * TB, ff)
        for m in range(dm // 256):
            at = pl.ds(m * 256, 256)
            got = lax.dot_general(
                left[:, m * 256 : (m + 1) * 256], right, (((0,), (0,)), ((), ())),
                preferred_element_type=F32,
            )
            if not opening:
                got = got + acc[at, :]
            if closing:
                gw_out[at, :] = got.astype(BF16)
            else:
                acc[at, :] = got

    def collect(h):
        pltpu.make_async_copy(rs_in.at[h], rs_in.at[h], rs_recv.at[h]).wait()
        total = rs_in[h, 0].astype(F32)
        for j in range(1, 16):
            total = total + rs_in[h, j].astype(F32)
        gt_out[pl.ds(h * TB, TB), :] = total.astype(BF16)

    for c in range(AHEAD):
        send_tokens(c)

    def stage(i, offset, fn):
        c = i - offset

        @pl.when((c >= 0) & (c < NC))
        def _():
            fn(jnp.clip(c, 0, NC - 1))

    def step(i, _):
        stage(i, 0, first)
        for s in (1, 2, 3):
            stage(i, s, lambda c: ring_step(c, s))
        stage(i, 4, middle)
        for s in (1, 2, 3):
            stage(i, 4 + s, lambda c: gath_step(c, s))
        stage(i, 8, back)
        stage(i, 9, scatter)

        @pl.when(i == 9)
        def _():
            weigh(0, 2, True, False)

        @pl.when(i == 11)
        def _():
            weigh(2, 2, False, False)

        return 0

    lax.fori_loop(0, NC + 8, step, 0)
    weigh(4, 4, False, True)
    scatter(NC - 1)
    collect(0)
    collect(1)

    for h in range(2):
        sent = rs_in.at[h, pl.ds(0, 15)]
        pltpu.make_async_copy(sent, sent, tok_send.at[h]).wait()

    def drain(c, _):
        for d in range(2):
            for s in range(4):
                ring_copy(d, c, s).wait_send()
                gath_copy(d, c, s).wait_send()
        mine = core == lax.rem(c, 2)

        @pl.when(mine)
        def _():
            forward_tokens(c).wait_send()

        @pl.when(mine & (r_me == lax.rem(c, 4)))
        def _():
            sent = quo_in.at[c, pl.ds(0, 7)]
            pltpu.make_async_copy(sent, sent, rs_send.at[c]).wait()

        @pl.when(mine & (r_me != lax.rem(c, 4)))
        def _():
            sent = quo_in.at[c]
            pltpu.make_async_copy(sent, sent, rs_send.at[c]).wait()

        @pl.when(jnp.logical_not(mine))
        def _():
            quo_copy(c).wait_send()

        return 0

    lax.fori_loop(0, NC, drain, 0)


def local(tokens, weight, grad_out):
    dm, ff = weight.shape
    dma = pltpu.SemaphoreType.DMA
    vmem = pltpu.VMEM
    return pl.pallas_call(
        kernel,
        out_shape=(
            jax.ShapeDtypeStruct(grad_out.shape, BF16),
            jax.ShapeDtypeStruct(tokens.shape, BF16),
            jax.ShapeDtypeStruct(weight.shape, BF16),
        ),
        in_specs=[pl.BlockSpec(memory_space=pl.ANY)] * 3,
        out_specs=[pl.BlockSpec(memory_space=pltpu.VMEM)] * 3,
        scratch_shapes=[
            vmem((dm, ff), BF16),
            vmem(grad_out.shape, BF16),
            vmem((NC, NZ, TB, dm), BF16),
            vmem((NC, NZ, TB, ff), BF16),
            vmem((2, NC, 4, TB, ff), BF16),
            vmem((NC, NZ, TB, ff), BF16),
            vmem((NC, NZ, TB, dm), BF16),
            vmem((NC, NZ, TB, dm), BF16),
            vmem((2, 16, TB, dm), BF16),
            vmem((dm, ff), F32),
            dma((2,)), dma((NC,)), dma((NC,)),
            dma((2, NC, 4)), dma((2, NC, 4)), dma((2, NC, 4)), dma((2, NC, 4)),
            dma((NC,)), dma((NC,)), dma((NC,)), dma((2,)), dma((2,)),
        ],
        compiler_params=pltpu.CompilerParams(
            collective_id=0, has_side_effects=True, vmem_limit_bytes=60 * 1024 * 1024
        ),
        cost_estimate=pl.CostEstimate(
            flops=6 * 1024 * dm * ff, bytes_accessed=4 * dm * ff, transcendentals=0
        ),
        name="mlp",
    )(tokens, weight, grad_out)


def solution(mesh):
    placed = (P("row", "col"), P("col", "row"), P("col", "row"))
    return jax.shard_map(
        local,
        mesh=mesh,
        in_specs=placed,
        out_specs=(P("col", "row"), P("row", "col"), P("col", "row")),
        check_vma=False,
    )
```

time: 269 us -> 159 us (0.59)
  waiting for transfers between devices: 214 us -> 0 us
  Pallas kernels: 0 us -> 148 us
  matrix products: 27.2 us -> 0 us
  between operations: 13.8 us -> 0.64 us
    pallas_call x0 -> x1, Pallas kernels: none -> 148 us  [local(): pl.pallas_call(kernel, out_shape=(jax.ShapeDtypeStruct(grad_out.shape, BF...]
    reduce_scatter x2 -> x0, waiting for transfers between devices: 111 us -> none  [the longest x1 67.5 us: local(): lax.psum_scatter(rounded(times_transposed(rows, weight)).astype(jnp.bfloa...]
    all_gather x2 -> x0, waiting for transfers between devices: 102 us -> none  [the longest x1 55.7 us: local(): all_tokens = lax.all_gather(tokens, 'row', axis=0, tiled=True)]
    dot_general x3 -> x0, matrix products: 27.2 us -> none  [the longest x1 9.25 us: times_transposed(): lax.dot_general(left, right, (((1,), (1,)), ((), ())), preferred_element_...]
    unnamed x5 -> x3, local copies, waits for them, and re-layouts: 8.53 us -> 8.13 us
  transfers between devices with their start and end apart: 4 -> 0, of which waited for: 4 -> 0; matrix products, arithmetic and copies ran while one was open for 6% -> 0% of each run, Pallas kernels for 0% -> 0%
where the time goes in v1:
time: 159 us; the launch traced here: 157 us
  Pallas kernels  148 us (93%)
  local copies, waits for them, and re-layouts  8.13 us (5%)
    pallas_call x1, Pallas kernels, local(): pl.pallas_call(kernel, out_shape=(jax.ShapeDtypeStruct(grad_out.shape, BF...  148 us
    unnamed x3, local copies, waits for them, and re-layouts  8.13 us

profile of v1, /device:TPU:3, one launch (start us, length us, event | category | flops | bytes accessed | tf_op | source)
XLA Modules:
  0.0 156.9 jit_solution(16731223278186886083)
XLA Ops:
  0.6 148.1 %mlp.1 = (bf16[128,1536]{1,0:T(8,128)(2,1)}, bf16[32,1536]{1,0:T(8,128)(2,1)}, bf16[1536,1536]{1,0:T(8,128)(2,1)}) custom-call(bf16[32,1536]{1,0:T(8,128)(2,1)} %tok_in.1, bf16[1536,1536]{1,0:T(8,128)(2,1)} %w_in.1, bf16[128,1536]{1,0:T(8,128)(2,1)} %go_in.1), custom_call_target="tpu_custom_call" | custom-call | flops 14495514624 | bytes 9437184 | tf_op jit(solution)/shard_map/mlp/pallas_call | solution.py:319
  148.8 1.8 %copy.9 = bf16[128,1536]{1,0:T(8,128)(2,1)} copy(bf16[128,1536]{1,0:T(8,128)(2,1)} %get-tuple-element.6) | data formatting | bytes 786432
  150.6 1.5 copy.10
  152.1 4.8 %copy.11 = bf16[1536,1536]{1,0:T(8,128)(2,1)} copy(bf16[1536,1536]{1,0:T(8,128)(2,1)} %get-tuple-element.8) | data formatting | bytes 9437184

commit v2 on v1

v2 whole, which is shorter than its diff:
```python
import math

import jax
import jax.numpy as jnp
from jax import lax
from jax.experimental import pallas as pl
from jax.experimental.pallas import tpu as pltpu
from jax.sharding import PartitionSpec as P

MESH = pl.DeviceIdType.MESH
F32 = jnp.float32
BF16 = jnp.bfloat16
NZ = 8
NC = 8
TB = 16
AHEAD = 2


def activations(pre):
    coef = math.sqrt(2.0 / math.pi)
    inner = coef * (pre + 0.044715 * pre * pre * pre)
    tval = jnp.tanh(inner)
    hidden = 0.5 * pre * (1.0 + tval)
    slope = 0.5 * (1.0 + tval) + 0.5 * pre * (1.0 - tval * tval) * coef * (
        1.0 + 3.0 * 0.044715 * pre * pre
    )
    return (hidden, slope)


def kernel(
    tok_in, w_in, go_in,
    hid_out, gt_out, gw_out,
    w, wt, go, tok, part, ring, gath, quo, quo_in, rs_in, acc,
    tok_send, tok_recv, fwd_send, fwd_recv, ring_send, ring_recv, gath_send, gath_recv,
    quo_send, quo_recv, rs_send, rs_recv, load_sem,
):
    row = lax.axis_index("row")
    z = lax.axis_index("col")
    core = lax.rem(row, 2)
    chip = row // 2
    x, y = chip // 4, lax.rem(chip, 4)
    d_me, r_me = row // 4, lax.rem(row, 4)
    sibling = (row + 1 - 2 * core, z)
    hops = ((row, lax.rem(z + 1, NZ)), (row, lax.rem(z + NZ - 1, NZ)))
    k_me = lax.rem(r_me // 2 + d_me // 2, 2) + 2 * lax.rem(r_me + d_me, 2)
    dm = tok.shape[-1]
    ff = gath.shape[-1]
    half = ff // 2

    load_w = pltpu.make_async_copy(w_in, w, load_sem.at[0])
    load_go = pltpu.make_async_copy(go_in, go, load_sem.at[1])
    load_w.start()
    load_go.start()

    def plane(j):
        px = lax.rem(x + j // 4, 4)
        py = lax.rem(y + lax.rem(j, 4), 4)
        return ((px * 4 + py) * 2 + core, z)

    barrier = pltpu.get_barrier_semaphore()
    for there in (*hops, sibling):
        pl.semaphore_signal(barrier, inc=1, device_id=there, device_id_type=MESH)

    def greet(j, _):
        pl.semaphore_signal(barrier, inc=1, device_id=plane(j), device_id_type=MESH)
        return 0

    lax.fori_loop(1, 16, greet, 0)
    pl.semaphore_wait(barrier, 18)

    def slot(d):
        d = lax.rem(d, NZ)
        return lax.rem(d, 2) * 4 + d // 2

    def owner(c, d):
        k = lax.rem(c, 4)
        return 2 * lax.rem(k + d // 2, 2) + lax.rem(k // 2 + d, 2)

    def parity(c, of):
        return lax.rem(of + lax.rem(c, 4) // 2, 2)

    def four(c, of):
        return pl.ds(parity(c, of) * 4, 4)

    def remote(src, dst, send, recv, there):
        return pltpu.make_async_remote_copy(
            src_ref=src, dst_ref=dst, send_sem=send, recv_sem=recv,
            device_id=there, device_id_type=MESH,
        )

    def send_tokens(c):
        h = c // 4

        @pl.when(k_me == lax.rem(c, 4))
        def _():
            mine = tok_in.at[pl.ds(pl.multiple_of(h * TB, TB), TB)]

            def one(j, _):
                remote(mine, tok.at[c, slot(d_me)], tok_send.at[h], tok_recv.at[c], plane(j)).start()
                return 0

            lax.fori_loop(1, 16, one, 0)
            pltpu.make_async_copy(mine, tok.at[c, slot(d_me)], tok_recv.at[c]).start()

    def forward_tokens(c):
        part_of = tok.at[c, four(c, core)]
        return remote(part_of, part_of, fwd_send.at[c], fwd_recv.at[c], sibling)

    def ring_copy(d, c, s):
        if s == 0:
            cols = pl.ds(d * half, half)
            src = part.at[c, slot(z + 4), :, cols]
            dst = ring.at[d, c, 0, :, cols]
        else:
            src, dst = ring.at[d, c, s - 1], ring.at[d, c, s]
        return remote(src, dst, ring_send.at[d, c, s], ring_recv.at[d, c, s], hops[d])

    def gath_copy(d, c, s):
        at = slot(z + (NZ - s if d == 0 else s))
        if s == 3:
            ref = gath.at[c, at, :, pl.ds(d * half, half)]
        else:
            ref = gath.at[c, at]
        return remote(ref, ref, gath_send.at[d, c, s], gath_recv.at[d, c, s], hops[d])

    def fetch(c):
        direct = tok.at[c, four(c, core)]
        pltpu.make_async_copy(direct, direct, tok_recv.at[c]).wait()
        forward_tokens(c).start()

        @pl.when(c + AHEAD < NC)
        def _():
            send_tokens(c + AHEAD)

    def first(c):
        other = tok.at[c, four(c, 1 - core)]
        pltpu.make_async_copy(other, other, fwd_recv.at[c]).wait()
        left = tok[c].reshape(NZ * TB, dm)
        for n in range(ff // 256):
            at = pl.ds(n * 256, 256)
            got = jnp.dot(left, w[:, at], preferred_element_type=F32)
            part[c, :, :, at] = got.astype(BF16).reshape(NZ, TB, 256)
        for d in range(2):
            ring_copy(d, c, 0).start()

    def ring_step(c, s):
        for d in range(2):
            ring_copy(d, c, s - 1).wait_recv()
            at = slot(z + (4 - s if d == 0 else 4 + s))
            if s == 1:
                got, rest = slice(d * half, (d + 1) * half), slice((1 - d) * half, (2 - d) * half)
                total = ring[d, c, 0, :, got].astype(F32) + part[c, at, :, got].astype(F32)
                ring[d, c, 0, :, got] = total.astype(BF16)
                ring[d, c, 0, :, rest] = part[c, at, :, rest]
            else:
                total = ring[d, c, s - 1].astype(F32) + part[c, at].astype(F32)
                ring[d, c, s - 1] = total.astype(BF16)
            ring_copy(d, c, s).start()

    def middle(c):
        @pl.when(c == 0)
        def _():
            load_go.wait()

        for d in range(2):
            ring_copy(d, c, 3).wait_recv()
        at = pl.ds(pl.multiple_of(owner(c, z) * 32 + (c // 4) * TB, TB), TB)
        pre = (
            part[c, slot(z)].astype(F32) + ring[0, c, 3].astype(F32) + ring[1, c, 3].astype(F32)
        )
        hidden, slope = activations(pre)
        hid_out[at, :] = hidden.astype(BF16)
        gath[c, slot(z)] = (go[at, :].astype(F32) * slope).astype(BF16)
        for d in range(2):
            gath_copy(d, c, 0).start()

    def gath_step(c, s):
        for d in range(2):
            gath_copy(d, c, s - 1).wait_recv()
            gath_copy(d, c, s).start()

    def quo_copy(c):
        theirs = quo.at[c, four(c, 1 - core)]
        return remote(theirs, quo_in.at[c], quo_send.at[c], quo_recv.at[c], sibling)

    def back(c):
        for d in range(2):
            gath_copy(d, c, 3).wait_recv()
        left = gath[c].reshape(NZ * TB, ff)

        for n in range(dm // 256):
            at = pl.ds(n * 256, 256)
            got = jnp.dot(left, wt[:, at], preferred_element_type=F32)
            quo[c, :, :, at] = got.astype(BF16).reshape(NZ, TB, 256)
        quo_copy(c).start()

    def scatter(c):
        h, p = c // 4, parity(c, core)
        quo_copy(c).wait_recv()

        def one(j, _):
            at = lax.rem(d_me // 2 + j, 4)
            d = 2 * at + p
            mine = quo.at[c, p * 4 + at]
            total = quo[c, p * 4 + at].astype(F32) + quo_in[c, at].astype(F32)
            quo[c, p * 4 + at] = total.astype(BF16)
            there = d * 4 + owner(c, d)

            @pl.when(there != row)
            def _():
                remote(
                    mine, rs_in.at[h, chip], rs_send.at[c], rs_recv.at[h], (there, z)
                ).start()

            @pl.when(there == row)
            def _():
                pltpu.make_async_copy(mine, rs_in.at[h, chip], rs_recv.at[h]).start()

            return 0

        lax.fori_loop(0, 4, one, 0)

    def weigh(c, n, opening, closing, tiles):
        def tile(m, _):
            at = pl.ds(pl.multiple_of(m * 256, 256), 256)
            left = tok[pl.ds(c, n), :, :, at].reshape(n * NZ * TB, 256)
            for f in range(ff // 512):
                cols = pl.ds(f * 512, 512)
                right = gath[pl.ds(c, n), :, :, cols].reshape(n * NZ * TB, 512)
                got = lax.dot_general(
                    left, right, (((0,), (0,)), ((), ())), preferred_element_type=F32
                )
                if not opening:
                    got = got + acc[at, cols]
                if closing:
                    gw_out[at, cols] = got.astype(BF16)
                else:
                    acc[at, cols] = got
            return 0

        lax.fori_loop(tiles[0], tiles[1], tile, 0)

    def collect(h):
        pltpu.make_async_copy(rs_in.at[h], rs_in.at[h], rs_recv.at[h]).wait()
        total = rs_in[h, 0].astype(F32)
        for j in range(1, 16):
            total = total + rs_in[h, j].astype(F32)
        gt_out[pl.ds(h * TB, TB), :] = total.astype(BF16)

    def turn(n, _):
        at = pl.ds(pl.multiple_of(n * 256, 256), 256)
        wt[:, at] = w[at, :].T
        return 0

    for c in range(AHEAD):
        send_tokens(c)
    load_w.wait()
    lax.fori_loop(0, 4, turn, 0)
    fetch(0)
    lax.fori_loop(4, 6, turn, 0)

    def stage(i, offset, fn):
        c = i - offset

        @pl.when((c >= 0) & (c < NC))
        def _():
            fn(jnp.clip(c, 0, NC - 1))

    def step(i, _):
        stage(i, 1, lambda c: ring_step(c, 1))
        stage(i, 0, first)
        for s in (2, 3):
            stage(i, s, lambda c: ring_step(c, s))
        stage(i, 4, middle)
        for s in (1, 2, 3):
            stage(i, 4 + s, lambda c: gath_step(c, s))
        stage(i, 9, scatter)
        stage(i, 8, back)

        @pl.when(i == 9)
        def _():
            weigh(0, 2, True, False, (0, 6))

        @pl.when(i == 11)
        def _():
            weigh(2, 2, False, False, (0, 6))

        @pl.when(i + 1 < NC)
        def _():
            fetch(i + 1)

        return 0

    lax.fori_loop(0, NC + 8, step, 0)
    weigh(4, 4, False, True, (0, 2))
    scatter(NC - 1)
    weigh(4, 4, False, True, (2, 6))
    collect(0)
    collect(1)

    for h in range(2):
        sent = rs_in.at[h, pl.ds(0, 15)]
        pltpu.make_async_copy(sent, sent, tok_send.at[h]).wait()

    def drain(c, _):
        for d in range(2):
            for s in range(4):
                ring_copy(d, c, s).wait_send()
                gath_copy(d, c, s).wait_send()
        forward_tokens(c).wait_send()
        quo_copy(c).wait_send()

        @pl.when(k_me == lax.rem(c, 4))
        def _():
            sent = quo_in.at[c, pl.ds(0, 3)]
            pltpu.make_async_copy(sent, sent, rs_send.at[c]).wait()

        @pl.when(k_me != lax.rem(c, 4))
        def _():
            sent = quo_in.at[c]
            pltpu.make_async_copy(sent, sent, rs_send.at[c]).wait()

        return 0

    lax.fori_loop(0, NC, drain, 0)


def store(hid, gt, gw, hid_out, gt_out, gw_out, sem):
    copies = [
        pltpu.make_async_copy(src, dst, sem.at[n])
        for n, (src, dst) in enumerate(((gw, gw_out), (hid, hid_out), (gt, gt_out)))
    ]
    for copy in copies:
        copy.start()
    for copy in copies:
        copy.wait()


def local(tokens, weight, grad_out):
    dm, ff = weight.shape
    dma = pltpu.SemaphoreType.DMA
    vmem = pltpu.VMEM
    shapes = (grad_out.shape, tokens.shape, weight.shape)
    held = pl.pallas_call(
        kernel,
        out_shape=tuple(pltpu.VMEM(shape, BF16) for shape in shapes),
        in_specs=[pl.BlockSpec(memory_space=pl.ANY)] * 3,
        out_specs=[pl.BlockSpec(memory_space=pltpu.VMEM)] * 3,
        scratch_shapes=[
            vmem((dm, ff), BF16),
            vmem((ff, dm), BF16),
            vmem(grad_out.shape, BF16),
            vmem((NC, NZ, TB, dm), BF16),
            vmem((NC, NZ, TB, ff), BF16),
            vmem((2, NC, 4, TB, ff), BF16),
            vmem((NC, NZ, TB, ff), BF16),
            vmem((NC, NZ, TB, dm), BF16),
            vmem((NC, 4, TB, dm), BF16),
            vmem((2, 16, TB, dm), BF16),
            vmem((dm, ff), F32),
            dma((2,)), dma((NC,)), dma((NC,)), dma((NC,)),
            dma((2, NC, 4)), dma((2, NC, 4)), dma((2, NC, 4)), dma((2, NC, 4)),
            dma((NC,)), dma((NC,)), dma((NC,)), dma((2,)), dma((2,)),
        ],
        compiler_params=pltpu.CompilerParams(
            collective_id=0, has_side_effects=True, vmem_limit_bytes=56 * 1024 * 1024
        ),
        cost_estimate=pl.CostEstimate(
            flops=6 * 1024 * dm * ff, bytes_accessed=4 * dm * ff, transcendentals=0
        ),
        name="mlp",
    )(tokens, weight, grad_out)
    return pl.pallas_call(
        store,
        out_shape=tuple(jax.ShapeDtypeStruct(shape, BF16) for shape in shapes),
        in_specs=[pl.BlockSpec(memory_space=pltpu.VMEM)] * 3,
        out_specs=[pl.BlockSpec(memory_space=pl.ANY)] * 3,
        scratch_shapes=[dma((3,))],
        compiler_params=pltpu.CompilerParams(vmem_limit_bytes=1024 * 1024),
        name="store",
    )(*(pltpu.with_memory_space_constraint(x, pltpu.VMEM) for x in held))


def solution(mesh):
    placed = (P("row", "col"), P("col", "row"), P("col", "row"))
    return jax.shard_map(
        local,
        mesh=mesh,
        in_specs=placed,
        out_specs=(P("col", "row"), P("row", "col"), P("col", "row")),
        check_vma=False,
    )
```

time: 159 us -> 110 us (0.69); the launches traced: 157 us -> 110 us
  Pallas kernels: 148 us -> 109 us
  local copies, waits for them, and re-layouts: 8.13 us -> 0 us
    pallas_call x1 -> x2, Pallas kernels: 148 us -> 109 us  [the longest x1 107 us: local(): pl.pallas_call(kernel, out_shape=tuple((pltpu.VMEM(shape, BF16) for shape...]
    unnamed x3 -> x0, local copies, waits for them, and re-layouts: 8.13 us -> none
where the time goes in v2:
time: 110 us
  Pallas kernels  109 us (99%)
    pallas_call x1, Pallas kernels, local(): pl.pallas_call(kernel, out_shape=tuple((pltpu.VMEM(shape, BF16) for shape...  107 us
    pallas_call x1, Pallas kernels, local(): pl.pallas_call(store, out_shape=tuple((jax.ShapeDtypeStruct(shape, BF16)...  2.34 us

profile of v2, /device:TPU:3, one launch (start us, length us, event | category | flops | bytes accessed | tf_op | source)
XLA Modules:
  0.0 109.6 jit_solution(2588077356541615194)
XLA Ops:
  0.6 106.6 %mlp.1 = (bf16[128,1536]{1,0:T(8,128)(2,1)S(1)}, bf16[32,1536]{1,0:T(8,128)(2,1)S(1)}, bf16[1536,1536]{1,0:T(8,128)(2,1)S(1)}) custom-call(bf16[32,1536]{1,0:T(8,128)(2,1)} %tok_in.1, bf16[1536,1536]{1,0:T(8,128)(2,1)} %w_in.1, bf16[128,1536]{1,0:T(8,128)(2,1)} %go_in.1), custom_call_target="tpu_custom_call" | custom-call | flops 14495514624 | bytes 9437184 | tf_op jit(solution)/shard_map/mlp/pallas_call | solution.py:344
  107.2 2.3 %store.1 = (bf16[128,1536]{1,0:T(8,128)(2,1)}, bf16[32,1536]{1,0:T(8,128)(2,1)}, bf16[1536,1536]{1,0:T(8,128)(2,1)}) custom-call(bf16[128,1536]{1,0:T(8,128)(2,1)S(1)} %get-tuple-element.6.hid, bf16[32,1536]{1,0:T(8,128)(2,1)S(1)} %get-tuple-element.7.gt, bf16[1536,1536]{1,0:T(8,128)(2,1)S(1)} %get-tuple-element.8.gw), custom_call_target="tpu_custom_call" | custom-call | tf_op jit(solution)/shard_map/store/pallas_call | solution.py:373

commit v3 on v2

--- a/solution.py
+++ b/solution.py
@@ -13,7 +13,26 @@
 NZ = 8
 NC = 8
 TB = 16
-AHEAD = 2
+AHEAD = 3
+
+FAR_FIRST = (10, 9, 11, 8, 6, 14, 2, 5, 13, 7, 15, 4, 12, 1, 3)
+PLAN = (
+    (11, 3), (11, 4), (11, 5), (10, 0), (0, 0), (10, 1), (0, 1), (10, 2),
+    (1, 0), (0, 2), (10, 3), (1, 1), (2, 0), (0, 3), (10, 4), (1, 2),
+    (2, 1), (3, 0), (0, 4), (10, 5), (1, 3), (2, 2), (3, 1), (0, 5),
+    (10, 6), (4, 0), (1, 4), (2, 3), (3, 2), (10, 7), (0, 6), (4, 1),
+    (1, 5), (5, 0), (0, 7), (2, 4), (3, 3), (4, 2), (1, 6), (5, 1),
+    (2, 5), (6, 0), (1, 7), (3, 4), (4, 3), (5, 2), (2, 6), (6, 1),
+    (3, 5), (7, 0), (2, 7), (4, 4), (5, 3), (6, 2), (3, 6), (7, 1),
+    (4, 5), (8, 0), (3, 7), (5, 4), (6, 3), (9, 0), (7, 2), (4, 6),
+    (8, 1), (5, 5), (12, 0), (4, 7), (6, 4), (12, 1), (9, 1), (7, 3),
+    (8, 2), (5, 6), (12, 2), (6, 5), (12, 3), (5, 7), (12, 4), (9, 2),
+    (7, 4), (8, 3), (6, 6), (12, 5), (7, 5), (12, 6), (6, 7), (8, 4),
+    (9, 3), (7, 6), (8, 5), (9, 4), (7, 7), (12, 7), (12, 8), (8, 6),
+    (9, 5), (12, 9), (8, 7), (9, 6), (12, 10), (12, 11), (12, 12), (12, 13),
+    (9, 7), (12, 14), (12, 15), (12, 16), (12, 17), (12, 18), (12, 19), (12, 20),
+    (12, 21), (12, 22), (12, 23),
+)
 
 
 def activations(pre):
@@ -54,18 +73,15 @@
 
     def plane(j):
         px = lax.rem(x + j // 4, 4)
-        py = lax.rem(y + lax.rem(j, 4), 4)
+        py = lax.rem(y + j % 4, 4)
         return ((px * 4 + py) * 2 + core, z)
 
     barrier = pltpu.get_barrier_semaphore()
     for there in (*hops, sibling):
         pl.semaphore_signal(barrier, inc=1, device_id=there, device_id_type=MESH)
 
-    def greet(j, _):
+    for j in range(1, 16):
         pl.semaphore_signal(barrier, inc=1, device_id=plane(j), device_id_type=MESH)
-        return 0
-
-    lax.fori_loop(1, 16, greet, 0)
     pl.semaphore_wait(barrier, 18)
 
     def slot(d):
@@ -73,11 +89,11 @@
         return lax.rem(d, 2) * 4 + d // 2
 
     def owner(c, d):
-        k = lax.rem(c, 4)
+        k = c % 4
         return 2 * lax.rem(k + d // 2, 2) + lax.rem(k // 2 + d, 2)
 
     def parity(c, of):
-        return lax.rem(of + lax.rem(c, 4) // 2, 2)
+        return lax.rem(of + c % 4 // 2, 2)
 
     def four(c, of):
         return pl.ds(parity(c, of) * 4, 4)
@@ -91,15 +107,12 @@
     def send_tokens(c):
         h = c // 4
 
-        @pl.when(k_me == lax.rem(c, 4))
+        @pl.when(k_me == c % 4)
         def _():
             mine = tok_in.at[pl.ds(pl.multiple_of(h * TB, TB), TB)]
 
-            def one(j, _):
+            for j in FAR_FIRST:
                 remote(mine, tok.at[c, slot(d_me)], tok_send.at[h], tok_recv.at[c], plane(j)).start()
-                return 0
-
-            lax.fori_loop(1, 16, one, 0)
             pltpu.make_async_copy(mine, tok.at[c, slot(d_me)], tok_recv.at[c]).start()
 
     def forward_tokens(c):
@@ -128,8 +141,7 @@
         pltpu.make_async_copy(direct, direct, tok_recv.at[c]).wait()
         forward_tokens(c).start()
 
-        @pl.when(c + AHEAD < NC)
-        def _():
+        if c + AHEAD < NC:
             send_tokens(c + AHEAD)
 
     def first(c):
@@ -158,8 +170,7 @@
             ring_copy(d, c, s).start()
 
     def middle(c):
-        @pl.when(c == 0)
-        def _():
+        if c == 0:
             load_go.wait()
 
         for d in range(2):
@@ -198,8 +209,8 @@
         h, p = c // 4, parity(c, core)
         quo_copy(c).wait_recv()
 
-        def one(j, _):
-            at = lax.rem(d_me // 2 + j, 4)
+        def one(j):
+            at = lax.rem(x + j, 4)
             d = 2 * at + p
             mine = quo.at[c, p * 4 + at]
             total = quo[c, p * 4 + at].astype(F32) + quo_in[c, at].astype(F32)
@@ -216,29 +227,24 @@
             def _():
                 pltpu.make_async_copy(mine, rs_in.at[h, chip], rs_recv.at[h]).start()
 
-            return 0
-
-        lax.fori_loop(0, 4, one, 0)
-
-    def weigh(c, n, opening, closing, tiles):
-        def tile(m, _):
-            at = pl.ds(pl.multiple_of(m * 256, 256), 256)
-            left = tok[pl.ds(c, n), :, :, at].reshape(n * NZ * TB, 256)
-            for f in range(ff // 512):
-                cols = pl.ds(f * 512, 512)
-                right = gath[pl.ds(c, n), :, :, cols].reshape(n * NZ * TB, 512)
-                got = lax.dot_general(
-                    left, right, (((0,), (0,)), ((), ())), preferred_element_type=F32
-                )
-                if not opening:
-                    got = got + acc[at, cols]
-                if closing:
-                    gw_out[at, cols] = got.astype(BF16)
-                else:
-                    acc[at, cols] = got
-            return 0
-
-        lax.fori_loop(tiles[0], tiles[1], tile, 0)
+        for j in (2, 1, 3, 0):
+            one(j)
+
+    def weigh(pair, m):
+        at = pl.ds(m * 256, 256)
+        left = tok[pl.ds(2 * pair, 2), :, :, at].reshape(2 * NZ * TB, 256)
+        for f in range(ff // 512):
+            cols = pl.ds(f * 512, 512)
+            right = gath[pl.ds(2 * pair, 2), :, :, cols].reshape(2 * NZ * TB, 512)
+            got = lax.dot_general(
+                left, right, (((0,), (0,)), ((), ())), preferred_element_type=F32
+            )
+            if pair > 0:
+                got = got + acc[at, cols]
+            if 2 * pair + 2 == NC:
+                gw_out[at, cols] = got.astype(BF16)
+            else:
+                acc[at, cols] = got
 
     def collect(h):
         pltpu.make_async_copy(rs_in.at[h], rs_in.at[h], rs_recv.at[h]).wait()
@@ -247,54 +253,36 @@
             total = total + rs_in[h, j].astype(F32)
         gt_out[pl.ds(h * TB, TB), :] = total.astype(BF16)
 
-    def turn(n, _):
-        at = pl.ds(pl.multiple_of(n * 256, 256), 256)
+    def turn(n):
+        at = pl.ds(n * 256, 256)
         wt[:, at] = w[at, :].T
-        return 0
-
-    for c in range(AHEAD):
-        send_tokens(c)
+
+    send_tokens(0)
     load_w.wait()
-    lax.fori_loop(0, 4, turn, 0)
-    fetch(0)
-    lax.fori_loop(4, 6, turn, 0)
-
-    def stage(i, offset, fn):
-        c = i - offset
-
-        @pl.when((c >= 0) & (c < NC))
-        def _():
-            fn(jnp.clip(c, 0, NC - 1))
-
-    def step(i, _):
-        stage(i, 1, lambda c: ring_step(c, 1))
-        stage(i, 0, first)
-        for s in (2, 3):
-            stage(i, s, lambda c: ring_step(c, s))
-        stage(i, 4, middle)
-        for s in (1, 2, 3):
-            stage(i, 4 + s, lambda c: gath_step(c, s))
-        stage(i, 9, scatter)
-        stage(i, 8, back)
-
-        @pl.when(i == 9)
-        def _():
-            weigh(0, 2, True, False, (0, 6))
-
-        @pl.when(i == 11)
-        def _():
-            weigh(2, 2, False, False, (0, 6))
-
-        @pl.when(i + 1 < NC)
-        def _():
-            fetch(i + 1)
-
-        return 0
-
-    lax.fori_loop(0, NC + 8, step, 0)
-    weigh(4, 4, False, True, (0, 2))
-    scatter(NC - 1)
-    weigh(4, 4, False, True, (2, 6))
+    turn(0)
+    send_tokens(1)
+    turn(1)
+    turn(2)
+    send_tokens(2)
+    for kind, c in PLAN:
+        if kind == 0:
+            first(c)
+        elif kind < 4:
+            ring_step(c, kind)
+        elif kind == 4:
+            middle(c)
+        elif kind < 8:
+            gath_step(c, kind - 4)
+        elif kind == 8:
+            back(c)
+        elif kind == 9:
+            scatter(c)
+        elif kind == 10:
+            fetch(c)
+        elif kind == 11:
+            turn(c)
+        else:
+            weigh(c // 6, c % 6)
     collect(0)
     collect(1)
 
@@ -302,7 +290,7 @@
         sent = rs_in.at[h, pl.ds(0, 15)]
         pltpu.make_async_copy(sent, sent, tok_send.at[h]).wait()
 
-    def drain(c, _):
+    def drain(c):
         for d in range(2):
             for s in range(4):
                 ring_copy(d, c, s).wait_send()
@@ -310,19 +298,18 @@
         forward_tokens(c).wait_send()
         quo_copy(c).wait_send()
 
-        @pl.when(k_me == lax.rem(c, 4))
+        @pl.when(k_me == c % 4)
         def _():
             sent = quo_in.at[c, pl.ds(0, 3)]
             pltpu.make_async_copy(sent, sent, rs_send.at[c]).wait()
 
-        @pl.when(k_me != lax.rem(c, 4))
+        @pl.when(k_me != c % 4)
         def _():
             sent = quo_in.at[c]
             pltpu.make_async_copy(sent, sent, rs_send.at[c]).wait()
 
-        return 0
-
-    lax.fori_loop(0, NC, drain, 0)
+    for c in range(NC):
+        drain(c)
 
 
 def store(hid, gt, gw, hid_out, gt_out, gw_out, sem):

time: 110 us -> 106 us (0.964)
  Pallas kernels: 109 us -> 106 us
    pallas_call x1, Pallas kernels: 107 us -> 103 us  [local(): pl.pallas_call(kernel, out_shape=tuple((pltpu.VMEM(shape, BF16) for shape...]
where the time goes in v3:
time: 106 us
  Pallas kernels  106 us (100%)
    pallas_call x1, Pallas kernels, local(): pl.pallas_call(kernel, out_shape=tuple((pltpu.VMEM(shape, BF16) for shape...  103 us
    pallas_call x1, Pallas kernels, local(): pl.pallas_call(store, out_shape=tuple((jax.ShapeDtypeStruct(shape, BF16)...  2.34 us

profile of v3, /device:TPU:3, one launch (start us, length us, event | category | flops | bytes accessed | tf_op | source)
XLA Modules:
  0.0 106.3 jit_solution(2336607019657290567)
XLA Ops:
  0.6 103.2 %mlp.1 = (bf16[128,1536]{1,0:T(8,128)(2,1)S(1)}, bf16[32,1536]{1,0:T(8,128)(2,1)S(1)}, bf16[1536,1536]{1,0:T(8,128)(2,1)S(1)}) custom-call(bf16[32,1536]{1,0:T(8,128)(2,1)} %tok_in.1, bf16[1536,1536]{1,0:T(8,128)(2,1)} %w_in.1, bf16[128,1536]{1,0:T(8,128)(2,1)} %go_in.1), custom_call_target="tpu_custom_call" | custom-call | flops 14495514624 | bytes 9437184 | tf_op jit(solution)/shard_map/mlp/pallas_call | solution.py:331
  103.8 2.3 %store.1 = (bf16[128,1536]{1,0:T(8,128)(2,1)}, bf16[32,1536]{1,0:T(8,128)(2,1)}, bf16[1536,1536]{1,0:T(8,128)(2,1)}) custom-call(bf16[128,1536]{1,0:T(8,128)(2,1)S(1)} %get-tuple-element.6.hid, bf16[32,1536]{1,0:T(8,128)(2,1)S(1)} %get-tuple-element.7.gt, bf16[1536,1536]{1,0:T(8,128)(2,1)S(1)} %get-tuple-element.8.gw), custom_call_target="tpu_custom_call" | custom-call | tf_op jit(solution)/shard_map/store/pallas_call | solution.py:360
